TPU v7x, 512 devices: a whole 4x8x8 slice. The times are simulated.
512 devices in a mesh: snap: 8 (over z), tile: 64 (over x, y, core).
Axes of the slice: x: 4, y: 8, z: 8, core: 2. Of those that a mesh axis runs over, the one named last changes fastest.
Arguments:
- modes: bfloat16 [8192, 256], P(('snap', 'tile')), may hold values from -8 to 8
- targets: bfloat16 [8192, 256], P(('snap', 'tile')), may hold values from -16 to 16
- pairs: int32 [4096, 2], replicated, may hold values from 0 to 256, as said below
- support: int32 [4096, 256], P(('snap', 'tile')), may hold values from 0 to 1, as said below
Outputs:
- coeffs: float32 [4096, 256], P(('snap', 'tile'))
- resid: float32 [4096, 256], P(('snap', 'tile'))
Inputs may be any that keep to these rules, and one draw needn't show every extreme that they name: Rows are distinct unordered pairs; the first entry is below 256; every index below 256 is the first entry of exactly 16 rows. `support`: every target has at least one active term.
All inputs are finite; a program needn't handle non-finite values.
Results may differ from a plain program's by a relative error of at most 0.0036.
Values may be sent and summed in bfloat16 or wider, within the bound.
A program may use at most 64 MiB of HBM per device.

v0:
```python
import jax
import jax.numpy as jnp
from jax import lax
from jax.sharding import PartitionSpec as P

ITERS = 2


def widened(rows_in):
    return jnp.concatenate(
        [rows_in.astype(jnp.float32), jnp.ones((rows_in.shape[0], 1), jnp.float32)], axis=1
    )


def body(modes, targets, pairs, support):
    snap_count = lax.axis_size("snap")
    tile_count = lax.axis_size("tile")
    term_count = pairs.shape[0]
    mode_count = modes.shape[1]
    target_count = targets.shape[1]
    share_rows = term_count // (snap_count * tile_count)
    total_snaps = modes.shape[0] * snap_count * tile_count
    tile_at = lax.axis_index("tile")
    term_grid = jnp.arange(term_count, dtype=jnp.int32).reshape(snap_count, tile_count, share_rows)
    own_terms = lax.dynamic_index_in_dim(term_grid, tile_at, 1, keepdims=False).reshape(-1)
    first_factor = pairs[:, 0]
    second_factor = pairs[:, 1]
    start_sums = (
        jnp.zeros((snap_count * share_rows, term_count), jnp.float32),
        jnp.zeros((snap_count * share_rows, target_count), jnp.float32),
    )
    rows_in = lax.all_gather(modes, "tile", axis=0, tiled=True)
    count_rows = rows_in.shape[0]
    block_rows = max((divisor for divisor in range(1, 513) if count_rows % divisor == 0))

    def inner(totals, block_item):
        block_modes, block_targets = block_item
        extended = widened(block_modes)
        library = (
            jnp.take(extended, first_factor, axis=1) * jnp.take(extended, second_factor, axis=1)
        ).astype(jnp.bfloat16)
        mine = jnp.take(library, own_terms, axis=1)
        gram_sum = totals[0] + lax.dot_general(
            mine, library, (((0,), (0,)), ((), ())), preferred_element_type=jnp.float32
        )
        cross_sum = totals[1] + lax.dot_general(
            mine, block_targets, (((0,), (0,)), ((), ())), preferred_element_type=jnp.float32
        )
        return ((gram_sum, cross_sum), None)

    blocks = (
        rows_in.reshape(count_rows // block_rows, block_rows, mode_count),
        lax.all_gather(targets, "tile", axis=0, tiled=True).reshape(
            count_rows // block_rows, block_rows, target_count
        ),
    )
    results, _ = lax.scan(inner, start_sums, blocks)
    gram_part, cross_part = results
    gram_all, cross_all = lax.psum((gram_part, cross_part), "snap")
    snap_at = lax.axis_index("snap")
    gram_rows = lax.dynamic_slice_in_dim(gram_all, snap_at * share_rows, share_rows, 0)
    cross_rows = lax.dynamic_slice_in_dim(cross_all, snap_at * share_rows, share_rows, 0)
    gram_rows = gram_rows / total_snaps
    cross_rows = cross_rows / total_snaps
    support_mask = support.astype(jnp.float32)

    def energy_of(vector):
        return lax.psum(jnp.sum(vector * vector, axis=0), ("snap", "tile"))

    resid = support_mask * cross_rows
    coeffs = jnp.zeros_like(resid)
    direction = resid
    energy = energy_of(resid)
    for step in range(ITERS):
        product = jnp.dot(
            gram_rows,
            lax.all_gather(direction, ("snap", "tile"), axis=0, tiled=True),
            precision=lax.Precision.HIGHEST,
            preferred_element_type=jnp.float32,
        )
        image = support_mask * product
        step_len = energy / lax.psum(jnp.sum(direction * image, axis=0), ("snap", "tile"))
        coeffs = coeffs + step_len * direction
        resid = resid - step_len * image
        if step + 1 < ITERS:
            fresh = energy_of(resid)
            direction = resid + fresh / energy * direction
            energy = fresh
    return (coeffs, resid)


def solution(mesh):
    return jax.shard_map(
        body,
        mesh=mesh,
        in_specs=(
            P(("snap", "tile"), None),
            P(("snap", "tile"), None),
            P(),
            P(("snap", "tile"), None),
        ),
        out_specs=(P(("snap", "tile"), None), P(("snap", "tile"), None)),
        check_vma=False,
    )
```

profile of v0, /device:TPU:1, one launch (start us, length us, event | category | flops | bytes accessed | tf_op | source)
XLA Modules:
  0.0 834.8 jit_solution(8397565621540414149)
XLA Ops:
  7.2 0.0 all-reduce.5.cloned.1.call-start
  7.2 0.1 reshape.63
  7.3 0.9 fusion.16
  8.2 54.4 %all_gather.12 = bf16[1024,256]{1,0:T(8,128)(2,1)S(1)} all-gather(bf16[16,256]{1,0:T(8,128)(2,1)} %param.8), channel_id=1, replica_groups=mesh['snap'=8,'tile'=64] {'tile'}, dimensions={0}, use_global_device_ids=true | all-gather | bytes 532480 | tf_op jit(solution)/shard_map/all_gather | solution.py:32
  62.6 49.5 %all_gather.13 = bf16[1024,256]{1,0:T(8,128)(2,1)S(1)} all-gather(bf16[16,256]{1,0:T(8,128)(2,1)} %param.9), channel_id=1, replica_groups=mesh['snap'=8,'tile'=64] {'tile'}, dimensions={0}, use_global_device_ids=true | all-gather | bytes 532480 | tf_op jit(solution)/shard_map/all_gather | solution.py:53
  112.0 0.0 copy-start.4
  112.0 101.3 %while.13 = (s32[]{:T(128)}, f32[64,4096]{1,0:T(8,128)S(1)}, f32[64,256]{1,0:T(8,128)S(1)}, s32[64]{0:T(128)S(1)}, bf16[2,512,256]{2,1,0:T(8,128)(2,1)S(1)}, /*i...) while((s32[]{:T(128)}, f32[64,4096]{1,0:T(8,128)S(1)}, ...), condition=%wide.region_1.3_spmd.clone, body=%wide.region_0.2_spmd.clone.sunk | while | flops 294438976 | bytes 63463412 | solution.py:57
  112.1 0.1 copy.9
  112.2 0.1 pad_convert_fusion.2
  112.3 16.9 %gather_fusion.1 = f32[4096,512]{1,0:T(8,128)} fusion(f32[512,257]{0,1:T(8,128)S(1)} %pad_convert_fusion.2, s32[4096]{0:T(1024)S(1)} %get-tuple-element.170), kind=kCustom, calls=%fused_computation.clone.clone.1 | custom fusion | bytes 16793600 | tf_op jit(solution)/shard_map/while/body/eval_jaxpr/jit(_take)/gather | solution.py:40
  129.2 16.9 %gather_fusion = f32[4096,512]{1,0:T(8,128)} fusion(f32[512,257]{0,1:T(8,128)S(1)} %pad_convert_fusion.2, s32[4096]{0:T(1024)S(1)} %get-tuple-element.169), kind=kCustom, calls=%fused_computation.1.clone.clone.1 | custom fusion | bytes 16793600 | tf_op jit(solution)/shard_map/while/body/eval_jaxpr/jit(_take)/gather | solution.py:40
  146.1 9.2 %fusion.28 = bf16[512,4096]{0,1:T(8,128)(2,1)} fusion(f32[4096,512]{1,0:T(8,128)} %gather_fusion, f32[4096,512]{1,0:T(8,128)} %gather_fusion.1, pred[4096]{0:T(1024)(128)(4,1)S(1)} %get-tuple-element.171, pred[4096]{0:T(1024)(128)(4,1)S(1)} %get-tuple-element.172), kind=kLoop, calls=%fused_computation.4.clone.1 | loop fusion | flops 8388608 | bytes 20979712 | tf_op jit(solution)/shard_map/while/body/eval_jaxpr/convert_element_type | solution.py:41
  155.3 3.4 gather_fusion.2
  158.8 3.7 convolution_add_fusion.4
  162.4 0.2 convolution_add_fusion.5
  162.7 0.1 copy.9
  162.9 0.1 pad_convert_fusion.2
  163.0 16.9 %gather_fusion.1 = f32[4096,512]{1,0:T(8,128)} fusion(f32[512,257]{0,1:T(8,128)S(1)} %pad_convert_fusion.2, s32[4096]{0:T(1024)S(1)} %get-tuple-element.170), kind=kCustom, calls=%fused_computation.clone.clone.1 | custom fusion | bytes 16793600 | tf_op jit(solution)/shard_map/while/body/eval_jaxpr/jit(_take)/gather | solution.py:40
  179.8 16.9 %gather_fusion = f32[4096,512]{1,0:T(8,128)} fusion(f32[512,257]{0,1:T(8,128)S(1)} %pad_convert_fusion.2, s32[4096]{0:T(1024)S(1)} %get-tuple-element.169), kind=kCustom, calls=%fused_computation.1.clone.clone.1 | custom fusion | bytes 16793600 | tf_op jit(solution)/shard_map/while/body/eval_jaxpr/jit(_take)/gather | solution.py:40
  196.7 9.2 %fusion.28 = bf16[512,4096]{0,1:T(8,128)(2,1)} fusion(f32[4096,512]{1,0:T(8,128)} %gather_fusion, f32[4096,512]{1,0:T(8,128)} %gather_fusion.1, pred[4096]{0:T(1024)(128)(4,1)S(1)} %get-tuple-element.171, pred[4096]{0:T(1024)(128)(4,1)S(1)} %get-tuple-element.172), kind=kLoop, calls=%fused_computation.4.clone.1 | loop fusion | flops 8388608 | bytes 20979712 | tf_op jit(solution)/shard_map/while/body/eval_jaxpr/convert_element_type | solution.py:41
  205.9 3.4 gather_fusion.2
  209.4 3.7 convolution_add_fusion.4
  213.1 0.2 convolution_add_fusion.5
  213.3 0.0 copy-start
  213.3 0.0 copy-start.1
  213.4 1.0 copy-done
  214.3 0.0 copy-done.1
  214.4 0.0 all-reduce.5.cloned.1.call-update
  214.4 0.0 all-gather.3.cloned.1.call-start
  214.4 77.7 %all-reduce.5.cloned.1.call-done = (f32[64,256]{1,0:T(8,128)}, f32[64,4096]{1,0:T(8,128)}) async-done(((f32[64,256]{1,0:T(8,128)}, f32[64,4096]{1,0:T(8,128)}), (f32[64,256]{1,0:T(8,128)}, f32[64,4096]{1,0:T(8,128)})) %all-reduce.5.cloned.1.call-update) | async-done | bytes 1114128 | tf_op jit(solution)/shard_map/psum | solution.py:59
  292.2 0.0 copy-done.4
  292.2 1.3 multiply_multiply_fusion
  293.5 0.0 copy-start.2
  293.5 0.0 all-gather.3.cloned.1.call-update
  293.5 0.0 all-gather.5.cloned.1.call-start
  293.5 124.9 %all-gather.3.cloned.1.call-done = f32[4096,256]{1,0:T(8,128)} async-done(((f32[8,256]{1,0:T(8,128)}), f32[4096,256]{1,0:T(8,128)}) %all-gather.3.cloned.1.call-update) | async-done | bytes 4194320 | tf_op jit(solution)/shard_map/all_gather | solution.py:77
  418.5 3.9 multiply_reduce_fusion.2
  422.4 96.1 %all-reduce.1 = (f32[256]{0:T(256)S(1)}, f32[256]{0:T(256)S(1)}) all-reduce(f32[256]{0:T(256)S(1)} %get-tuple-element.84, f32[256]{0:T(256)S(1)} %get-tuple-element.83), channel_id=1, replica_groups=mesh['snap'=8,'tile'=64] {'snap','tile'}, use_global_device_ids=true, to_apply=%region_4.6 | all-reduce | flops 512 | bytes 4096 | tf_op jit(solution)/shard_map/psum | solution.py:68
  518.5 0.0 copy-done.2
  518.6 93.8 %psum.46 = f32[256]{0:T(256)S(1)} all-reduce(f32[256]{0:T(256)S(1)} %multiply_reduce_fusion.1), channel_id=1, replica_groups=mesh['snap'=8,'tile'=64] {'snap','tile'}, use_global_device_ids=true, to_apply=%region_9.11 | all-reduce | flops 256 | bytes 2048 | tf_op jit(solution)/shard_map/psum | solution.py:68
  612.4 0.6 multiply_add_fusion.1
  613.0 0.0 copy-start.3
  613.0 0.0 all-gather.5.cloned.1.call-update
  613.0 114.6 %all-gather.5.cloned.1.call-done = f32[4096,256]{1,0:T(8,128)} async-done(((f32[8,256]{1,0:T(8,128)}), f32[4096,256]{1,0:T(8,128)}) %all-gather.5.cloned.1.call-update) | async-done | bytes 4194320 | tf_op jit(solution)/shard_map/all_gather | solution.py:77
  727.6 3.9 multiply_reduce_fusion
  731.5 96.2 %psum.47 = f32[256]{0:T(256)S(1)} all-reduce(f32[256]{0:T(256)S(1)} %get-tuple-element.114), channel_id=1, replica_groups=mesh['snap'=8,'tile'=64] {'snap','tile'}, use_global_device_ids=true, to_apply=%region_11.13 | all-reduce | flops 256 | bytes 2048 | tf_op jit(solution)/shard_map/psum | solution.py:82
  827.7 0.0 copy-done.3
  827.7 0.6 multiply_subtract_fusion
  (19 shorter events, 0.2 us)
Async XLA Ops:
  7.2 285.0 %all-reduce.5.cloned.1.call-start = ((), (), s32[]{:S(2)}) async-start(), calls=%async_computation.2 | async-start | bytes 2228224 | tf_op jit(solution)/shard_map/psum | solution.py:59
  112.0 180.1 %copy-start.4 = (s32[8,256]{1,0:T(8,128)S(1)}, s32[8,256]{1,0:T(8,128)}, u32[]{:S(2)}) copy-start(s32[8,256]{1,0:T(8,128)} %param.11) | copy-start | bytes 24580
  213.3 1.0 copy-start
  213.3 1.0 copy-start.1
  214.4 204.1 %all-gather.3.cloned.1.call-start = ((), (), s32[]{:S(2)}) async-start(), calls=%async_computation | async-start | bytes 4202496 | tf_op jit(solution)/shard_map/all_gather | solution.py:77
  293.5 225.1 %copy-start.2 = (f32[8,256]{1,0:T(8,128)S(1)}, f32[8,256]{1,0:T(8,128)}, u32[]{:S(2)}) copy-start(f32[8,256]{1,0:T(8,128)} %multiply_multiply_fusion) | copy-start | bytes 24580
  293.5 434.1 %all-gather.5.cloned.1.call-start = ((), (), s32[]{:S(2)}) async-start(), calls=%async_computation.1 | async-start | bytes 4202496 | tf_op jit(solution)/shard_map/all_gather | solution.py:77
  613.0 214.7 %copy-start.3 = (f32[8,256]{1,0:T(8,128)S(1)}, f32[8,256]{1,0:T(8,128)}, u32[]{:S(2)}) copy-start(f32[8,256]{1,0:T(8,128)} %multiply_add_fusion.1) | copy-start | bytes 24580
Sparse Core Ops, SparseCore 0:
  214.5 77.6 all-reduce.4
  297.6 120.7 all-gather.2
  613.1 114.4 all-gather.4
where the time goes:
time: 835 us
  blocking collectives  390 us (47%)
  waiting for transfers between devices  317 us (38%)
  local copies, waits for them, and re-layouts  76.7 us (9%)
  other arithmetic  21.2 us (3%)
  matrix products  15.7 us (2%)
  between operations  13.8 us (2%)
    all_gather x2, waiting for transfers between devices, body(): lax.all_gather(direction, ('snap', 'tile'), axis=0, tiled=True)  239 us
    psum x2, blocking collectives, energy_of(): return lax.psum(jnp.sum(vector * vector, axis=0), ('snap', 'tile'))  190 us
    psum x1, blocking collectives, body(): lax.psum(jnp.sum(direction * image, axis=0), ('snap', 'tile'))  96.2 us
    psum x1, waiting for transfers between devices, body(): gram_all, cross_all = lax.psum((gram_part, cross_part), 'snap')  77.7 us
    all_gather x1, blocking collectives, body(): rows_in = lax.all_gather(modes, 'tile', axis=0, tiled=True)  54.4 us
    all_gather x1, blocking collectives, body(): lax.all_gather(targets, 'tile', axis=0, tiled=True)  49.5 us
    gather x2, local copies, waits for them, and re-layouts, inner(): jnp.take(extended, first_factor, axis=1)  33.8 us
    gather x2, local copies, waits for them, and re-layouts, inner(): jnp.take(extended, second_factor, axis=1)  33.7 us
  transfers between devices with their start and end apart: 3, of which 3 were waited for; matrix products, arithmetic and copies ran while one was open for 0% of the time, Pallas kernels for 0%

commit v1 on v0

--- a/solution.py
+++ b/solution.py
@@ -65,7 +65,7 @@
     support_mask = support.astype(jnp.float32)
 
     def energy_of(vector):
-        return lax.psum(jnp.sum(vector * vector, axis=0), ("snap", "tile"))
+        return jnp.sum(lax.all_gather(jnp.sum(vector * vector, axis=0), ("snap", "tile")), axis=0)
 
     resid = support_mask * cross_rows
     coeffs = jnp.zeros_like(resid)

time: 835 us -> 875 us (1.048)
  blocking collectives: 390 us -> 430 us
    psum x2 -> x0, blocking collectives: 190 us -> none  [energy_of(): return lax.psum(jnp.sum(vector * vector, axis=0), ('snap', 'tile'))]
    all_gather x0 -> x2, blocking collectives: none -> 134 us  [energy_of(): lax.all_gather(jnp.sum(vector * vector, axis=0), ('snap', 'tile'))]
    psum x1 -> x2, blocking collectives: 96.2 us -> 191 us  [body(): lax.psum(jnp.sum(direction * image, axis=0), ('snap', 'tile'))]
where the time goes in v1:
time: 875 us; the launch traced here: 874 us
  blocking collectives  430 us (49%)
  waiting for transfers between devices  316 us (36%)
  local copies, waits for them, and re-layouts  76.3 us (9%)
  other arithmetic  22.3 us (3%)
  matrix products  15.7 us (2%)
  between operations  13.8 us (2%)
    all_gather x2, waiting for transfers between devices, body(): lax.all_gather(direction, ('snap', 'tile'), axis=0, tiled=True)  239 us
    psum x2, blocking collectives, body(): lax.psum(jnp.sum(direction * image, axis=0), ('snap', 'tile'))  191 us
    all_gather x2, blocking collectives, energy_of(): lax.all_gather(jnp.sum(vector * vector, axis=0), ('snap', 'tile'))  134 us
    psum x1, waiting for transfers between devices, body(): gram_all, cross_all = lax.psum((gram_part, cross_part), 'snap')  77.7 us
    all_gather x1, blocking collectives, body(): rows_in = lax.all_gather(modes, 'tile', axis=0, tiled=True)  54.4 us
    all_gather x1, blocking collectives, body(): lax.all_gather(targets, 'tile', axis=0, tiled=True)  49.5 us
    gather x2, local copies, waits for them, and re-layouts, inner(): jnp.take(extended, first_factor, axis=1)  33.6 us
    gather x2, local copies, waits for them, and re-layouts, inner(): jnp.take(extended, second_factor, axis=1)  33.6 us
  transfers between devices with their start and end apart: 3, of which 3 were waited for; matrix products, arithmetic and copies ran while one was open for 0% of the time, Pallas kernels for 0%

profile of v1, /device:TPU:1, one launch (start us, length us, event | category | flops | bytes accessed | tf_op | source)
XLA Modules:
  0.0 874.4 jit_solution(2667893897141048627)
XLA Ops:
  7.2 0.0 all-reduce.4.cloned.1.call-start
  7.2 0.1 reshape.67
  7.3 0.9 fusion.16
  8.2 54.4 %all_gather.24 = bf16[1024,256]{1,0:T(8,128)(2,1)S(1)} all-gather(bf16[16,256]{1,0:T(8,128)(2,1)} %param.8), channel_id=1, replica_groups=mesh['snap'=8,'tile'=64] {'tile'}, dimensions={0}, use_global_device_ids=true | all-gather | bytes 532480 | tf_op jit(solution)/shard_map/all_gather | solution.py:32
  62.6 49.5 %all_gather.25 = bf16[1024,256]{1,0:T(8,128)(2,1)S(1)} all-gather(bf16[16,256]{1,0:T(8,128)(2,1)} %param.9), channel_id=1, replica_groups=mesh['snap'=8,'tile'=64] {'tile'}, dimensions={0}, use_global_device_ids=true | all-gather | bytes 532480 | tf_op jit(solution)/shard_map/all_gather | solution.py:53
  112.0 0.0 copy-start.4
  112.0 101.0 %while.13 = (s32[]{:T(128)}, f32[64,4096]{1,0:T(8,128)S(1)}, f32[64,256]{1,0:T(8,128)S(1)}, s32[64]{0:T(128)S(1)}, bf16[2,512,256]{2,1,0:T(8,128)(2,1)S(1)}, /*i...) while((s32[]{:T(128)}, f32[64,4096]{1,0:T(8,128)S(1)}, ...), condition=%wide.region_1.3_spmd.clone, body=%wide.region_0.2_spmd.clone.sunk | while | flops 294438976 | bytes 63463412 | solution.py:57
  112.1 0.1 copy.10
  112.2 0.1 pad_convert_fusion.2
  112.3 16.8 %gather_fusion.1 = f32[4096,512]{1,0:T(8,128)} fusion(f32[512,257]{0,1:T(8,128)S(1)} %pad_convert_fusion.2, s32[4096]{0:T(1024)S(1)} %get-tuple-element.176), kind=kCustom, calls=%fused_computation.clone.clone.1 | custom fusion | bytes 16793600 | tf_op jit(solution)/shard_map/while/body/eval_jaxpr/jit(_take)/gather | solution.py:40
  129.1 16.8 %gather_fusion = f32[4096,512]{1,0:T(8,128)} fusion(f32[512,257]{0,1:T(8,128)S(1)} %pad_convert_fusion.2, s32[4096]{0:T(1024)S(1)} %get-tuple-element.175), kind=kCustom, calls=%fused_computation.1.clone.clone.1 | custom fusion | bytes 16793600 | tf_op jit(solution)/shard_map/while/body/eval_jaxpr/jit(_take)/gather | solution.py:40
  145.9 9.2 %fusion.28 = bf16[512,4096]{0,1:T(8,128)(2,1)} fusion(f32[4096,512]{1,0:T(8,128)} %gather_fusion, f32[4096,512]{1,0:T(8,128)} %gather_fusion.1, pred[4096]{0:T(1024)(128)(4,1)S(1)} %get-tuple-element.177, pred[4096]{0:T(1024)(128)(4,1)S(1)} %get-tuple-element.178), kind=kLoop, calls=%fused_computation.4.clone.1 | loop fusion | flops 8388608 | bytes 20979712 | tf_op jit(solution)/shard_map/while/body/eval_jaxpr/convert_element_type | solution.py:41
  155.1 3.4 gather_fusion.2
  158.6 3.7 convolution_add_fusion.4
  162.3 0.2 convolution_add_fusion.5
  162.6 0.1 copy.10
  162.7 0.1 pad_convert_fusion.2
  162.8 16.8 %gather_fusion.1 = f32[4096,512]{1,0:T(8,128)} fusion(f32[512,257]{0,1:T(8,128)S(1)} %pad_convert_fusion.2, s32[4096]{0:T(1024)S(1)} %get-tuple-element.176), kind=kCustom, calls=%fused_computation.clone.clone.1 | custom fusion | bytes 16793600 | tf_op jit(solution)/shard_map/while/body/eval_jaxpr/jit(_take)/gather | solution.py:40
  179.6 16.8 %gather_fusion = f32[4096,512]{1,0:T(8,128)} fusion(f32[512,257]{0,1:T(8,128)S(1)} %pad_convert_fusion.2, s32[4096]{0:T(1024)S(1)} %get-tuple-element.175), kind=kCustom, calls=%fused_computation.1.clone.clone.1 | custom fusion | bytes 16793600 | tf_op jit(solution)/shard_map/while/body/eval_jaxpr/jit(_take)/gather | solution.py:40
  196.4 9.2 %fusion.28 = bf16[512,4096]{0,1:T(8,128)(2,1)} fusion(f32[4096,512]{1,0:T(8,128)} %gather_fusion, f32[4096,512]{1,0:T(8,128)} %gather_fusion.1, pred[4096]{0:T(1024)(128)(4,1)S(1)} %get-tuple-element.177, pred[4096]{0:T(1024)(128)(4,1)S(1)} %get-tuple-element.178), kind=kLoop, calls=%fused_computation.4.clone.1 | loop fusion | flops 8388608 | bytes 20979712 | tf_op jit(solution)/shard_map/while/body/eval_jaxpr/convert_element_type | solution.py:41
  205.6 3.4 gather_fusion.2
  209.1 3.7 convolution_add_fusion.4
  212.8 0.2 convolution_add_fusion.5
  213.0 0.0 copy-start
  213.0 0.0 copy-start.1
  213.0 1.0 copy-done
  214.0 0.0 copy-done.1
  214.0 0.0 all-reduce.4.cloned.1.call-update
  214.1 0.0 all-gather.7.cloned.1.call-start
  214.1 77.7 %all-reduce.4.cloned.1.call-done = (f32[64,256]{1,0:T(8,128)}, f32[64,4096]{1,0:T(8,128)}) async-done(((f32[64,256]{1,0:T(8,128)}, f32[64,4096]{1,0:T(8,128)}), (f32[64,256]{1,0:T(8,128)}, f32[64,4096]{1,0:T(8,128)})) %all-reduce.4.cloned.1.call-update) | async-done | bytes 1114128 | tf_op jit(solution)/shard_map/psum | solution.py:59
  291.8 0.0 copy-done.4
  291.8 1.3 multiply_multiply_fusion
  293.1 0.0 copy-start.2
  293.1 0.0 all-gather.7.cloned.1.call-update
  293.2 0.0 all-gather.9.cloned.1.call-start
  293.2 124.9 %all-gather.7.cloned.1.call-done = f32[4096,256]{1,0:T(8,128)} async-done(((f32[8,256]{1,0:T(8,128)}), f32[4096,256]{1,0:T(8,128)}) %all-gather.7.cloned.1.call-update) | async-done | bytes 4194320 | tf_op jit(solution)/shard_map/all_gather | solution.py:77
  418.1 3.9 multiply_reduce_fusion.2
  422.1 67.5 %all-gather.2 = f32[512,1,256]{2,1,0:T(1,128)S(1)} all-gather(f32[1,1,256]{2,1,0:T(1,128)S(1)} %bitcast.45), channel_id=2, replica_groups=mesh['snap'=8,'tile'=64] {'snap','tile'}, dimensions={0}, use_global_device_ids=true | all-gather | bytes 525312 | tf_op jit(solution)/shard_map/all_gather | solution.py:68
  489.5 95.2 %psum.30 = f32[256]{0:T(256)S(1)} all-reduce(f32[256]{0:T(256)S(1)} %get-tuple-element.91), channel_id=1, replica_groups=mesh['snap'=8,'tile'=64] {'snap','tile'}, use_global_device_ids=true, to_apply=%region_7.9 | all-reduce | flops 256 | bytes 2048 | tf_op jit(solution)/shard_map/psum | solution.py:82
  584.8 0.6 reduce_sum.55
  585.4 0.0 copy-done.2
  585.4 66.9 %all-gather.3 = f32[512,1,256]{2,1,0:T(1,128)S(1)} all-gather(f32[1,1,256]{2,1,0:T(1,128)S(1)} %bitcast.44), channel_id=3, replica_groups=mesh['snap'=8,'tile'=64] {'snap','tile'}, dimensions={0}, use_global_device_ids=true | all-gather | bytes 525312 | tf_op jit(solution)/shard_map/all_gather | solution.py:68
  652.2 0.6 reduce_sum.58
  652.8 0.6 multiply_add_fusion.1
  653.4 0.0 copy-start.3
  653.4 0.0 all-gather.9.cloned.1.call-update
  653.4 113.7 %all-gather.9.cloned.1.call-done = f32[4096,256]{1,0:T(8,128)} async-done(((f32[8,256]{1,0:T(8,128)}), f32[4096,256]{1,0:T(8,128)}) %all-gather.9.cloned.1.call-update) | async-done | bytes 4194320 | tf_op jit(solution)/shard_map/all_gather | solution.py:77
  767.2 3.9 multiply_reduce_fusion
  771.1 96.2 %psum.31 = f32[256]{0:T(256)S(1)} all-reduce(f32[256]{0:T(256)S(1)} %get-tuple-element.120), channel_id=1, replica_groups=mesh['snap'=8,'tile'=64] {'snap','tile'}, use_global_device_ids=true, to_apply=%region_11.13 | all-reduce | flops 256 | bytes 2048 | tf_op jit(solution)/shard_map/psum | solution.py:82
  867.3 0.0 copy-done.3
  867.3 0.6 multiply_subtract_fusion
  (19 shorter events, 0.2 us)
Async XLA Ops:
  7.2 284.7 %all-reduce.4.cloned.1.call-start = ((), (), s32[]{:S(2)}) async-start(), calls=%async_computation.2 | async-start | bytes 2228224 | tf_op jit(solution)/shard_map/psum | solution.py:59
  112.0 179.8 %copy-start.4 = (s32[8,256]{1,0:T(8,128)S(1)}, s32[8,256]{1,0:T(8,128)}, u32[]{:S(2)}) copy-start(s32[8,256]{1,0:T(8,128)} %param.11) | copy-start | bytes 24580
  213.0 1.0 copy-start
  213.0 1.0 copy-start.1
  214.1 204.1 %all-gather.7.cloned.1.call-start = ((), (), s32[]{:S(2)}) async-start(), calls=%async_computation | async-start | bytes 4202496 | tf_op jit(solution)/shard_map/all_gather | solution.py:77
  293.1 292.2 %copy-start.2 = (f32[8,256]{1,0:T(8,128)S(1)}, f32[8,256]{1,0:T(8,128)}, u32[]{:S(2)}) copy-start(f32[8,256]{1,0:T(8,128)} %multiply_multiply_fusion) | copy-start | bytes 24580
  293.2 474.0 %all-gather.9.cloned.1.call-start = ((), (), s32[]{:S(2)}) async-start(), calls=%async_computation.1 | async-start | bytes 4202496 | tf_op jit(solution)/shard_map/all_gather | solution.py:77
  653.4 213.8 %copy-start.3 = (f32[8,256]{1,0:T(8,128)S(1)}, f32[8,256]{1,0:T(8,128)}, u32[]{:S(2)}) copy-start(f32[8,256]{1,0:T(8,128)} %multiply_add_fusion.1) | copy-start | bytes 24580
Sparse Core Ops, SparseCore 0:
  214.2 77.6 all-reduce.3
  297.3 120.7 all-gather.6
  653.6 113.5 all-gather.8
